TPU v7x, 1024 devices: a whole 4x8x16 slice. The times are simulated.
1024 devices in a mesh: blk: 32 (over x, z_lo), group: 32 (over y, z_hi, core).
Axes of the slice: x: 4, y: 8, z: 16 (z_hi: 2, z_lo: 8; z = z_hi * 8 + z_lo), core: 2. Of those that a mesh axis runs over, the one named last changes fastest.
Arguments:
- images: bfloat16 [163840, 1152], P(('blk', 'group')), may hold values from -4 to 4
- texts: bfloat16 [163840, 1152], P(('blk', 'group')), may hold values from -4 to 4
- exponent_of_multiplier: float32 [1], replicated, may hold values from 1 to 2
- bias: float32 [1], replicated, may hold values from -3 to -1
Outputs:
- grad_images: float32 [163840, 1152], P(('blk', 'group'))
- grad_texts: float32 [163840, 1152], P(('blk', 'group'))
- loss_mean: float32 [1], replicated
- temp_grad: float32 [1], replicated
- bias_grad: float32 [1], replicated
All inputs are finite; a program needn't handle non-finite values.
Results may differ from a plain program's by a relative error of at most 0.00055.
Values may be sent and summed in bfloat16 or wider, within the bound.
A program may use at most 32 MiB of HBM per device.

v0:
```python
import jax
import jax.numpy as jnp
from jax import lax
from jax.sharding import PartitionSpec as P

SHIFTS = 4


norm_eps = 1e-06


def passed_along(value, axis, steps):
    count = lax.axis_size(axis)
    pairs = [(source, (source + steps) % count) for source in range(count)]
    return lax.ppermute(value, axis, pairs)


def from_partner(array, axis, apart):
    return lax.ppermute(array, axis, [(i, i ^ 1 << apart) for i in range(lax.axis_size(axis))])


def prepare(rows):
    widened = rows.astype(jnp.float32)
    length = jnp.sqrt(jnp.sum(widened * widened, axis=-1, keepdims=True) + norm_eps)
    unit_rows = widened / length
    return (unit_rows, length, unit_rows.astype(jnp.bfloat16))


def unnormalize(unit_rows, length, gradient):
    along = jnp.sum(unit_rows * gradient, axis=-1, keepdims=True)
    return (gradient - unit_rows * along) / length


def visiting_text_block(
    picture_entry_segment,
    caption_entry_segment,
    inverse_sharpness,
    displaced_intercept,
    matching_indicator,
):
    angular_agreement = lax.dot_general(
        picture_entry_segment,
        caption_entry_segment,
        (((1,), (1,)), ((), ())),
        preferred_element_type=jnp.float32,
    )
    matching_scores = inverse_sharpness * angular_agreement + displaced_intercept
    if matching_indicator:
        label_sign = 2.0 * jnp.eye(angular_agreement.shape[0], dtype=jnp.float32) - 1.0
    else:
        label_sign = -jnp.ones_like(angular_agreement)
    flipped = -label_sign * matching_scores
    objective_aggregate = jnp.sum(jax.nn.softplus(flipped))
    logistic_derivatives = -label_sign * jax.nn.sigmoid(flipped)
    target_sign_factors = (inverse_sharpness * logistic_derivatives).astype(jnp.bfloat16)
    picture_derivative_share = jnp.dot(
        target_sign_factors, caption_entry_segment, preferred_element_type=jnp.float32
    )
    caption_derivative_share = lax.dot_general(
        target_sign_factors,
        picture_entry_segment,
        (((0,), (0,)), ((), ())),
        preferred_element_type=jnp.float32,
    )
    accumulated_sums = jnp.stack(
        [
            objective_aggregate,
            jnp.sum(logistic_derivatives * inverse_sharpness * angular_agreement),
            jnp.sum(logistic_derivatives),
        ]
    )
    return (picture_derivative_share, caption_derivative_share, accumulated_sums)


def body(images, texts, exponent_of_multiplier, bias):
    img_unit, img_len, picture_reduced_accuracy = prepare(images)
    txt_unit, txt_len, txt_bf = prepare(texts)
    row_count = images.shape[0]
    inverse_sharpness = jnp.exp(exponent_of_multiplier[0])
    displaced_intercept = bias[0]
    swap_bit = lax.axis_size("group").bit_length() - 2
    grad_img = jnp.zeros(img_unit.shape, jnp.float32)
    accumulated_sums = jnp.zeros((3,), jnp.float32)
    cycle_segments = txt_bf
    carried = jnp.zeros(txt_unit.shape, jnp.float32)
    for segment_displacement in range(SHIFTS):
        if segment_displacement > 0:
            cycle_segments, carried = (
                passed_along(cycle_segments.astype(jnp.float32), "blk", 1).astype(
                    cycle_segments.dtype
                ),
                passed_along(carried, "blk", 1),
            )
        picture_derivative_share, caption_derivative_share, interim_objective = visiting_text_block(
            picture_reduced_accuracy,
            cycle_segments,
            inverse_sharpness,
            displaced_intercept,
            segment_displacement == 0,
        )
        grad_img = grad_img + picture_derivative_share
        carried = carried + caption_derivative_share
        accumulated_sums = accumulated_sums + interim_objective
    cycle_segments, carried = (
        from_partner(cycle_segments.astype(jnp.float32), "group", swap_bit).astype(
            cycle_segments.dtype
        ),
        from_partner(carried, "group", swap_bit),
    )
    picture_derivative_share, caption_derivative_share, interim_objective = visiting_text_block(
        picture_reduced_accuracy, cycle_segments, inverse_sharpness, displaced_intercept, False
    )
    grad_img = grad_img + picture_derivative_share
    carried = carried + caption_derivative_share
    accumulated_sums = accumulated_sums + interim_objective
    carried = from_partner(carried, "group", swap_bit)
    carried = passed_along(carried, "blk", -(SHIFTS - 1))
    summed = lax.psum(accumulated_sums, ("blk", "group"))
    pair_count = (
        row_count * lax.axis_size("blk") * lax.axis_size("group") * (SHIFTS + 1) * row_count
    )
    scaled = summed / pair_count
    grad_images = unnormalize(img_unit, img_len, grad_img)
    grad_texts = unnormalize(txt_unit, txt_len, carried)
    return (grad_images, grad_texts, scaled[0:1], scaled[1:2], scaled[2:3])


def solution(mesh):
    in_specs = (P(("blk", "group"), None), P(("blk", "group"), None), P(), P())
    out_specs = (P(("blk", "group"), None), P(("blk", "group"), None), P(), P(), P())
    return jax.shard_map(body, mesh=mesh, in_specs=in_specs, out_specs=out_specs, check_vma=False)
```

profile of v0, /device:TPU:66, one launch (start us, length us, event | category | flops | bytes accessed | tf_op | source)
XLA Modules:
  0.0 352.6 jit_solution(6387029784086033439)
XLA Ops:
  0.7 1.2 fusion.2
  3.4 1.2 fusion.8
  5.0 4.3 %collective-permute-start.4 = (f32[160,1152]{1,0:T(8,128)S(1)}, f32[160,1152]{1,0:T(8,128)S(1)}, u32[]{:S(2)}, u32[]{:S(2)}) collective-permute-start(f32[160,1152]{1,0:T(8,128)S(1)} %fusion.13), channel_id=1, source_target_pairs={{0,32},{32,64},{64,96},{96,128},{128,160},{160,192},{192,224},{224... | collective-permute-start | bytes 2211848 | tf_op jit(solution)/shard_map/ppermute | solution.py:15
  9.4 4.3 %collective-permute-start = (bf16[160,1152]{1,0:T(8,128)(2,1)S(1)}, bf16[160,1152]{1,0:T(8,128)(2,1)S(1)}, u32[]{:S(2)}, u32[]{:S(2)}) collective-permute-start(bf16[160,1152]{1,0:T(8,128)(2,1)S(1)} %convert_convert_fusion.3), channel_id=1, source_target_pairs={{0,32},{32,64},{64,96},{96,128},{128,160},{160,192},{192,224},{224... | collective-permute-start | bytes 1105928 | tf_op jit(solution)/shard_map/ppermute | solution.py:15
  13.7 19.3 %collective-permute-done = bf16[160,1152]{1,0:T(8,128)(2,1)S(1)} collective-permute-done((bf16[160,1152]{1,0:T(8,128)(2,1)S(1)}, bf16[160,1152]{1,0:T(8,128)(2,1)S(1)}, u32[]{:S(2)}, u32[]{:S(2)}) %collective-permute-start) | collective-permute-done | bytes 368672 | tf_op jit(solution)/shard_map/ppermute | solution.py:15
  33.0 4.3 %collective-permute-start.1 = (bf16[160,1152]{1,0:T(8,128)(2,1)S(1)}, bf16[160,1152]{1,0:T(8,128)(2,1)S(1)}, u32[]{:S(2)}, u32[]{:S(2)}) collective-permute-start(bf16[160,1152]{1,0:T(8,128)(2,1)S(1)} %collective-permute-done), channel_id=1, source_target_pairs={{0,32},{32,64},{64,96},{96,128},{128,160},{160,192},{192,224},{224... | collective-permute-start | bytes 1105928 | tf_op jit(solution)/shard_map/ppermute | solution.py:15
  37.3 1.2 fusion.9
  38.8 5.4 %collective-permute-start.5 = (f32[160,1152]{1,0:T(8,128)S(1)}, f32[160,1152]{1,0:T(8,128)S(1)}, u32[]{:S(2)}, u32[]{:S(2)}) collective-permute-start(f32[160,1152]{1,0:T(8,128)S(1)} %convolution_add_fusion), channel_id=1, source_target_pairs={{0,32},{32,64},{64,96},{96,128},{128,160},{160,192},{192,224},{224... | collective-permute-start | bytes 2211848 | tf_op jit(solution)/shard_map/ppermute | solution.py:15
  44.2 12.5 %collective-permute-done.1 = bf16[160,1152]{1,0:T(8,128)(2,1)S(1)} collective-permute-done((bf16[160,1152]{1,0:T(8,128)(2,1)S(1)}, bf16[160,1152]{1,0:T(8,128)(2,1)S(1)}, u32[]{:S(2)}, u32[]{:S(2)}) %collective-permute-start.1) | collective-permute-done | bytes 368672 | tf_op jit(solution)/shard_map/ppermute | solution.py:15
  56.7 1.9 collective-permute-start.2
  58.6 1.2 fusion.10
  60.5 12.1 %collective-permute-done.5 = f32[160,1152]{1,0:T(8,128)S(1)} collective-permute-done((f32[160,1152]{1,0:T(8,128)S(1)}, f32[160,1152]{1,0:T(8,128)S(1)}, u32[]{:S(2)}, u32[]{:S(2)}) %collective-permute-start.5) | collective-permute-done | bytes 737312 | tf_op jit(solution)/shard_map/ppermute | solution.py:15
  72.6 1.9 collective-permute-start.6
  74.9 4.1 %collective-permute-done.2 = bf16[160,1152]{1,0:T(8,128)(2,1)S(1)} collective-permute-done((bf16[160,1152]{1,0:T(8,128)(2,1)S(1)}, bf16[160,1152]{1,0:T(8,128)(2,1)S(1)}, u32[]{:S(2)}, u32[]{:S(2)}) %collective-permute-start.2) | collective-permute-done | bytes 368672 | tf_op jit(solution)/shard_map/ppermute | solution.py:15
  78.9 7.7 %collective-permute-start.3 = (bf16[160,1152]{1,0:T(8,128)(2,1)S(1)}, bf16[160,1152]{1,0:T(8,128)(2,1)S(1)}, u32[]{:S(2)}, u32[]{:S(2)}) collective-permute-start(bf16[160,1152]{1,0:T(8,128)(2,1)S(1)} %collective-permute-done.2), channel_id=1, source_target_pairs={{0,16},{1,17},{2,18},{3,19},{4,20},{5,21},{6,22},{7,23},{8,24},{9,... | collective-permute-start | bytes 1105928 | tf_op jit(solution)/shard_map/ppermute | solution.py:19
  88.2 9.1 %collective-permute-done.6 = f32[160,1152]{1,0:T(8,128)S(1)} collective-permute-done((f32[160,1152]{1,0:T(8,128)S(1)}, f32[160,1152]{1,0:T(8,128)S(1)}, u32[]{:S(2)}, u32[]{:S(2)}) %collective-permute-start.6) | collective-permute-done | bytes 737312 | tf_op jit(solution)/shard_map/ppermute | solution.py:15
  97.3 7.7 %collective-permute-start.7 = (f32[160,1152]{1,0:T(8,128)S(1)}, f32[160,1152]{1,0:T(8,128)S(1)}, u32[]{:S(2)}, u32[]{:S(2)}) collective-permute-start(f32[160,1152]{1,0:T(8,128)S(1)} %add.127), channel_id=1, source_target_pairs={{0,16},{1,17},{2,18},{3,19},{4,20},{5,21},{6,22},{7,23},{8,24},{9,... | collective-permute-start | bytes 2211848 | tf_op jit(solution)/shard_map/ppermute | solution.py:19
  105.4 1.2 fusion.12
  106.6 9.5 %maximum_add_fusion.1 = f32[3]{0:T(128)S(1)} fusion(f32[1]{0:T(128)} %bitcast.16, f32[1]{0:T(128)} %bitcast.15, f32[1]{0:T(128)} %bitcast.14, f32[1]{0:T(128)} %bitcast.13, f32[1]{0:T(128)} %bitcast.12, f32[1]{0:T(128)} %bitcast.11, f32[1]{0:T(128)} %bitcast.10, f32[1]{0:T(128)} %bitcast.9, f32[1]{0:T(128)} %bitcast.8, f32[1]{0:T(128)} %bitcast.7, ...), kind=kLoop, calls=%fused_computation.62 | loop fusion | flops 42 | bytes 72 | tf_op jit(solution)/shard_map/add | solution.py:115
  116.4 20.2 %collective-permute-done.7 = f32[160,1152]{1,0:T(8,128)S(1)} collective-permute-done((f32[160,1152]{1,0:T(8,128)S(1)}, f32[160,1152]{1,0:T(8,128)S(1)}, u32[]{:S(2)}, u32[]{:S(2)}) %collective-permute-start.7) | collective-permute-done | bytes 737312 | tf_op jit(solution)/shard_map/ppermute | solution.py:19
  136.7 5.0 %collective-permute-start.8 = (f32[160,1152]{1,0:T(8,128)S(1)}, f32[160,1152]{1,0:T(8,128)}, u32[]{:S(2)}, u32[]{:S(2)}) collective-permute-start(f32[160,1152]{1,0:T(8,128)S(1)} %add.128), channel_id=1, source_target_pairs={{0,16},{1,17},{2,18},{3,19},{4,20},{5,21},{6,22},{7,23},{8,24},{9,... | collective-permute-start | bytes 2211848 | tf_op jit(solution)/shard_map/ppermute | solution.py:19
  141.9 153.0 %psum.7 = f32[3]{0:T(128)S(1)} all-reduce(f32[3]{0:T(128)S(1)} %maximum_add_fusion.1), channel_id=1, replica_groups=mesh['blk'=32,'group'=32] {'blk','group'}, use_global_device_ids=true, to_apply=%region_19.20 | all-reduce | flops 3 | bytes 24 | tf_op jit(solution)/shard_map/psum | solution.py:118
  296.4 1.9 collective-permute-start.9
  300.0 51.2 %collective-permute-done.9 = f32[160,1152]{1,0:T(8,128)S(1)} collective-permute-done((f32[160,1152]{1,0:T(8,128)}, f32[160,1152]{1,0:T(8,128)S(1)}, u32[]{:S(2)}, u32[]{:S(2)}) %collective-permute-start.9) | collective-permute-done | bytes 737312 | tf_op jit(solution)/shard_map/ppermute | solution.py:15
  (38 shorter events, 9.1 us)
Async XLA Ops:
  0.6 1.2 copy-start
  0.6 2.8 copy-start.1
  5.0 33.5 %collective-permute-start.4 = (f32[160,1152]{1,0:T(8,128)S(1)}, f32[160,1152]{1,0:T(8,128)S(1)}, u32[]{:S(2)}, u32[]{:S(2)}) collective-permute-start(f32[160,1152]{1,0:T(8,128)S(1)} %fusion.13), channel_id=1, source_target_pairs={{0,32},{32,64},{64,96},{96,128},{128,160},{160,192},{192,224},{224... | collective-permute-start | bytes 2211848 | tf_op jit(solution)/shard_map/ppermute | solution.py:15
  9.4 23.6 %collective-permute-start = (bf16[160,1152]{1,0:T(8,128)(2,1)S(1)}, bf16[160,1152]{1,0:T(8,128)(2,1)S(1)}, u32[]{:S(2)}, u32[]{:S(2)}) collective-permute-start(bf16[160,1152]{1,0:T(8,128)(2,1)S(1)} %convert_convert_fusion.3), channel_id=1, source_target_pairs={{0,32},{32,64},{64,96},{96,128},{128,160},{160,192},{192,224},{224... | collective-permute-start | bytes 1105928 | tf_op jit(solution)/shard_map/ppermute | solution.py:15
  33.0 23.7 %collective-permute-start.1 = (bf16[160,1152]{1,0:T(8,128)(2,1)S(1)}, bf16[160,1152]{1,0:T(8,128)(2,1)S(1)}, u32[]{:S(2)}, u32[]{:S(2)}) collective-permute-start(bf16[160,1152]{1,0:T(8,128)(2,1)S(1)} %collective-permute-done), channel_id=1, source_target_pairs={{0,32},{32,64},{64,96},{96,128},{128,160},{160,192},{192,224},{224... | collective-permute-start | bytes 1105928 | tf_op jit(solution)/shard_map/ppermute | solution.py:15
  38.8 33.7 %collective-permute-start.5 = (f32[160,1152]{1,0:T(8,128)S(1)}, f32[160,1152]{1,0:T(8,128)S(1)}, u32[]{:S(2)}, u32[]{:S(2)}) collective-permute-start(f32[160,1152]{1,0:T(8,128)S(1)} %convolution_add_fusion), channel_id=1, source_target_pairs={{0,32},{32,64},{64,96},{96,128},{128,160},{160,192},{192,224},{224... | collective-permute-start | bytes 2211848 | tf_op jit(solution)/shard_map/ppermute | solution.py:15
  56.7 3.1 copy-start.2
  56.7 22.2 %collective-permute-start.2 = (bf16[160,1152]{1,0:T(8,128)(2,1)S(1)}, bf16[160,1152]{1,0:T(8,128)(2,1)S(1)}, u32[]{:S(2)}, u32[]{:S(2)}) collective-permute-start(bf16[160,1152]{1,0:T(8,128)(2,1)S(1)} %collective-permute-done.1), channel_id=1, source_target_pairs={{0,32},{32,64},{64,96},{96,128},{128,160},{160,192},{192,224},{224... | collective-permute-start | bytes 1105928 | tf_op jit(solution)/shard_map/ppermute | solution.py:15
  59.8 0.7 copy-start.4
  72.6 24.7 %collective-permute-start.6 = (f32[160,1152]{1,0:T(8,128)S(1)}, f32[160,1152]{1,0:T(8,128)S(1)}, u32[]{:S(2)}, u32[]{:S(2)}) collective-permute-start(f32[160,1152]{1,0:T(8,128)S(1)} %add.126), channel_id=1, source_target_pairs={{0,32},{32,64},{64,96},{96,128},{128,160},{160,192},{192,224},{224... | collective-permute-start | bytes 2211848 | tf_op jit(solution)/shard_map/ppermute | solution.py:15
  78.9 26.4 %collective-permute-start.3 = (bf16[160,1152]{1,0:T(8,128)(2,1)S(1)}, bf16[160,1152]{1,0:T(8,128)(2,1)S(1)}, u32[]{:S(2)}, u32[]{:S(2)}) collective-permute-start(bf16[160,1152]{1,0:T(8,128)(2,1)S(1)} %collective-permute-done.2), channel_id=1, source_target_pairs={{0,16},{1,17},{2,18},{3,19},{4,20},{5,21},{6,22},{7,23},{8,24},{9,... | collective-permute-start | bytes 1105928 | tf_op jit(solution)/shard_map/ppermute | solution.py:19
  97.3 39.2 %collective-permute-start.7 = (f32[160,1152]{1,0:T(8,128)S(1)}, f32[160,1152]{1,0:T(8,128)S(1)}, u32[]{:S(2)}, u32[]{:S(2)}) collective-permute-start(f32[160,1152]{1,0:T(8,128)S(1)} %add.127), channel_id=1, source_target_pairs={{0,16},{1,17},{2,18},{3,19},{4,20},{5,21},{6,22},{7,23},{8,24},{9,... | collective-permute-start | bytes 2211848 | tf_op jit(solution)/shard_map/ppermute | solution.py:19
  136.7 159.8 %collective-permute-start.8 = (f32[160,1152]{1,0:T(8,128)S(1)}, f32[160,1152]{1,0:T(8,128)}, u32[]{:S(2)}, u32[]{:S(2)}) collective-permute-start(f32[160,1152]{1,0:T(8,128)S(1)} %add.128), channel_id=1, source_target_pairs={{0,16},{1,17},{2,18},{3,19},{4,20},{5,21},{6,22},{7,23},{8,24},{9,... | collective-permute-start | bytes 2211848 | tf_op jit(solution)/shard_map/ppermute | solution.py:19
  295.0 1.0 copy-start.3
  295.0 1.0 copy-start.5
  296.4 54.8 %collective-permute-start.9 = (f32[160,1152]{1,0:T(8,128)}, f32[160,1152]{1,0:T(8,128)S(1)}, u32[]{:S(2)}, u32[]{:S(2)}) collective-permute-start(f32[160,1152]{1,0:T(8,128)} %collective-permute-done.8), channel_id=1, source_target_pairs={{0,928},{32,960},{64,992},{96,0},{128,32},{160,64},{192,96},{224,1... | collective-permute-start | bytes 2211848 | tf_op jit(solution)/shard_map/ppermute | solution.py:15
where the time goes:
time: 353 us
  blocking collectives  153 us (43%)
  waiting for transfers between devices  128 us (36%)
  starting transfers between devices  44.4 us (13%)
  other arithmetic  13.6 us (4%)
  matrix products  9.22 us (3%)
    psum x1, blocking collectives, body(): summed = lax.psum(accumulated_sums, ('blk', 'group'))  153 us
    ppermute x7, waiting for transfers between devices, passed_along(): return lax.ppermute(value, axis, pairs)  108 us
    ppermute x7, starting transfers between devices, passed_along(): return lax.ppermute(value, axis, pairs)  24 us
    ppermute x3, starting transfers between devices, from_partner(): lax.ppermute(array, axis, [(i, i ^ 1 << apart) for i in range(lax.axis_si...  20.5 us
    ppermute x3, waiting for transfers between devices, from_partner(): lax.ppermute(array, axis, [(i, i ^ 1 << apart) for i in range(lax.axis_si...  20.2 us
    add x1, other arithmetic, body(): accumulated_sums = accumulated_sums + interim_objective  9.46 us
  transfers between devices with their start and end apart: 10, of which 7 were waited for; matrix products, arithmetic and copies ran while one was open for 5% of the time, Pallas kernels for 0%

commit v1 on v0

v1 whole, which is shorter than its diff:
```python
import functools

import jax
import jax.numpy as jnp
from jax import lax
from jax.experimental import pallas as pl
from jax.experimental.pallas import tpu as pltpu
from jax.sharding import PartitionSpec as P

MESH = pl.DeviceIdType.MESH
SHIFTS = 4
EPS = 1e-06
RUN = 8
CHUNK = 32
COLS = 384


def ring_stages(b, g, n_blk, n_group):
    x, zl = lax.div(b, RUN), lax.rem(b, RUN)
    y, low = lax.div(g, 4), lax.rem(g, 4)
    zh, core = lax.div(low, 2), lax.rem(low, 2)
    n_x, n_y = n_blk // RUN, n_group // 4
    z = zh * RUN + zl

    def along_z(k):
        other = lax.rem(z + k, 2 * RUN)
        return (x * RUN + lax.rem(other, RUN), y * 4 + lax.div(other, RUN) * 2 + core)

    return [
        (core, [(b, y * 4 + zh * 2 + (1 - core))]),
        (x, [(lax.rem(b + RUN * k, n_blk), g) for k in range(1, n_x)]),
        (y, [(b, lax.rem(g + 4 * k, n_group)) for k in range(1, n_y)]),
        (z, [along_z(k) for k in range(1, 2 * RUN)]),
    ]


def kernel(
    n_blk, n_group, scale_ref, images_ref, texts_ref,
    gimg_ref, gtxt_ref, sums_ref,
    blocks, unit, length, grad, totals, parts,
    send_sem, recv_sem, part_send, part_recv,
):
    rows, width = images_ref.shape
    n_chunks = rows // CHUNK
    b, g = lax.axis_index("blk"), lax.axis_index("group")
    right, left = lax.rem(b + 1, n_blk), lax.rem(b + n_blk - 1, n_blk)
    partner = lax.rem(g + n_group // 2, n_group)
    stages = ring_stages(b, g, n_blk, n_group)

    barrier = pltpu.get_barrier_semaphore()
    peers = [(right, g), (left, g), (b, partner)] + [p for _, line in stages for p in line]
    for peer in peers:
        pl.semaphore_signal(barrier, inc=1, device_id=peer, device_id_type=MESH)

    temperature = jnp.exp(scale_ref[0])
    bias = scale_ref[1]

    for stream, ref in ((0, texts_ref), (1, images_ref)):
        widened = ref[...].astype(jnp.float32)
        size = jnp.sqrt(jnp.sum(widened * widened, axis=-1, keepdims=True) + EPS)
        unit_rows = widened / size
        unit[stream] = unit_rows
        length[stream] = size
        blocks[stream, 0] = unit_rows.astype(jnp.bfloat16)
    totals[...] = jnp.zeros_like(totals)

    def move(stream, hop, chunk):
        last = lax.div(hop, SHIFTS - 1)
        to_blk = last * b + (1 - last) * (stream * left + (1 - stream) * right)
        to_group = last * partner + (1 - last) * g
        at = pl.ds(pl.multiple_of(chunk * CHUNK, CHUNK), CHUNK)
        return pltpu.make_async_remote_copy(
            src_ref=blocks.at[stream, hop, at],
            dst_ref=blocks.at[stream, hop + 1, at],
            send_sem=send_sem.at[stream, hop, chunk],
            recv_sem=recv_sem.at[stream, hop, chunk],
            device_id=(to_blk, to_group),
            device_id_type=MESH,
        )

    def meet(stream, hop, own, add):
        mine, block = blocks[1 - stream, 0], blocks[stream, hop]
        cosine = lax.dot_general(mine, block, (((1,), (1,)), ((), ())), preferred_element_type=jnp.float32)
        logits = temperature * cosine + bias
        if own:
            same = lax.broadcasted_iota(jnp.int32, (rows, rows), 0) == lax.broadcasted_iota(jnp.int32, (rows, rows), 1)
            sign = jnp.where(same, 1.0, -1.0)
            flipped = -sign * logits
        else:
            flipped = logits
        slope = jax.nn.sigmoid(flipped)
        if own:
            slope = -sign * slope
        weights = (temperature * slope).astype(jnp.bfloat16)
        for c in range(0, width, COLS):
            part = jnp.dot(weights, blocks[stream, hop, :, c : c + COLS], preferred_element_type=jnp.float32)
            if add:
                grad[1 - stream, :, c : c + COLS] += part
            else:
                grad[1 - stream, :, c : c + COLS] = part
        counted = 1.0 - jnp.asarray(stream, jnp.float32)
        term = jnp.maximum(flipped, 0.0) + jnp.log1p(jnp.exp(-jnp.abs(flipped)))
        for i, value in enumerate((term, slope * (temperature * cosine), slope)):
            totals[i : i + 1, :] += counted * jnp.sum(value, axis=0, keepdims=True)

    pl.semaphore_wait(barrier, len(peers))

    def first(chunk, carry):
        move(0, 0, chunk).start()
        move(1, 0, chunk).start()
        return carry

    lax.fori_loop(0, n_chunks, first, 0)
    meet(0, 0, True, False)
    meet(1, 0, True, False)

    place = lax.rem(b, RUN)
    high = lax.div(place, RUN // 2)
    edge = (1 - high) * place + high * (RUN - 1 - place)
    near = 1 - high

    def pick(k, table):
        value = jnp.int32(table[-1])
        for i in range(len(table) - 1):
            value = jnp.where(k == i, table[i], value)
        return value

    def visit(k, carry):
        far_0, far_1, far_2 = (pick(k, t) for t in ((0, 0, 0, 1, 1, 1, 0, 1), (0, 1, 0, 0, 1, 1, 0, 1), (0, 1, 0, 1, 0, 1, 0, 1)))
        hop_0, hop_1, hop_2 = (pick(k, t) for t in ((1, 2, 3, 1, 2, 3, 4, 4), (1, 1, 2, 3, 2, 3, 4, 4), (1, 1, 2, 2, 3, 3, 4, 4)))
        far = jnp.where(edge == 0, far_0, jnp.where(edge == 1, far_1, far_2))
        hop = jnp.where(edge == 0, hop_0, jnp.where(edge == 1, hop_1, hop_2))
        stream = far * (1 - near) + (1 - far) * near

        def take(chunk, c):
            move(stream, hop - 1, chunk).wait_recv()

            @pl.when(hop < SHIFTS)
            def _():
                move(stream, hop, chunk).start()

            return c

        lax.fori_loop(0, n_chunks, take, 0)
        meet(stream, hop, False, True)
        return carry

    lax.fori_loop(0, 2 * SHIFTS, visit, 0)

    sums = jnp.sum(totals[...], axis=1, keepdims=True)
    value = jnp.broadcast_to(sums, (8, 128))
    k = 0
    copies = []
    for s, (index, line) in enumerate(stages):
        parts[s, index] = value
        mine = []
        for peer in line:
            copy = pltpu.make_async_remote_copy(
                src_ref=parts.at[s, index],
                dst_ref=parts.at[s, index],
                send_sem=part_send.at[k],
                recv_sem=part_recv.at[k],
                device_id=peer,
                device_id_type=MESH,
            )
            copy.start()
            mine.append(copy)
            k += 1
        if s == 0:
            for stream, out in ((0, gtxt_ref), (1, gimg_ref)):
                gradient, unit_rows = grad[stream], unit[stream]
                along = jnp.sum(unit_rows * gradient, axis=-1, keepdims=True)
                out[...] = (gradient - unit_rows * along) / length[stream]
        for copy in mine:
            copy.wait_recv()
        value = parts[s, 0]
        for i in range(1, len(line) + 1):
            value = value + parts[s, i]
        copies += mine
    count = n_blk * n_group * rows * (SHIFTS + 1) * rows
    sums_ref[...] = value / count

    def sent(chunk, carry):
        for stream in (0, 1):
            for hop in range(SHIFTS):
                move(stream, hop, chunk).wait_send()
        return carry

    lax.fori_loop(0, n_chunks, sent, 0)
    for copy in copies:
        copy.wait_send()


def solution(mesh):
    n_blk, n_group = mesh.shape["blk"], mesh.shape["group"]

    def body(images, texts, exponent_of_multiplier, bias):
        rows, width = images.shape
        n_chunks = rows // CHUNK
        n_parts = 1 + (n_blk // RUN - 1) + (n_group // 4 - 1) + (2 * RUN - 1)
        scale = jnp.concatenate([exponent_of_multiplier, bias])
        vmem = pl.BlockSpec(memory_space=pltpu.VMEM)
        grad_images, grad_texts, sums = pl.pallas_call(
            functools.partial(kernel, n_blk, n_group),
            out_shape=[
                jax.ShapeDtypeStruct((rows, width), jnp.float32),
                jax.ShapeDtypeStruct((rows, width), jnp.float32),
                jax.ShapeDtypeStruct((8, 128), jnp.float32),
            ],
            in_specs=[pl.BlockSpec(memory_space=pltpu.SMEM), vmem, vmem],
            out_specs=[vmem, vmem, vmem],
            scratch_shapes=[
                pltpu.VMEM((2, SHIFTS + 1, rows, width), jnp.bfloat16),
                pltpu.VMEM((2, rows, width), jnp.float32),
                pltpu.VMEM((2, rows, 1), jnp.float32),
                pltpu.VMEM((2, rows, width), jnp.float32),
                pltpu.VMEM((8, rows), jnp.float32),
                pltpu.VMEM((4, 2 * RUN, 8, 128), jnp.float32),
                pltpu.SemaphoreType.DMA((2, SHIFTS, n_chunks)),
                pltpu.SemaphoreType.DMA((2, SHIFTS, n_chunks)),
                pltpu.SemaphoreType.DMA((n_parts,)),
                pltpu.SemaphoreType.DMA((n_parts,)),
            ],
            compiler_params=pltpu.CompilerParams(
                collective_id=0, has_side_effects=True, vmem_limit_bytes=48 * 2**20
            ),
        )(scale, images, texts)
        return grad_images, grad_texts, sums[0, 0:1], sums[1, 0:1], sums[2, 0:1]

    in_specs = (P(("blk", "group"), None), P(("blk", "group"), None), P(), P())
    out_specs = (P(("blk", "group"), None), P(("blk", "group"), None), P(), P(), P())
    return jax.shard_map(body, mesh=mesh, in_specs=in_specs, out_specs=out_specs, check_vma=False)
```

time: 353 us -> 126 us (0.36)
  the two profiles are of different devices: /device:TPU:66 before, /device:TPU:1 now
where the time goes in v1:
time: 126 us; the launch traced here: 125 us
  Pallas kernels  119 us (94%)
  local copies, waits for them, and re-layouts  4.22 us (3%)
  between operations  1.93 us (2%)
    pallas_call x1, Pallas kernels, body(): pl.pallas_call(functools.partial(kernel, n_blk, n_group), out_shape=[jax....  119 us
    unnamed x6, local copies, waits for them, and re-layouts  3.7 us

profile of v1, /device:TPU:1, one launch (start us, length us, event | category | flops | bytes accessed | tf_op | source)
XLA Modules:
  0.0 125.4 jit_solution(15744333723529761169)
XLA Ops:
  1.9 0.1 pad_maximum_fusion.scale_ref
  2.0 0.0 copy-start
  2.0 1.0 copy-done
  3.0 0.0 copy-start.1
  3.0 1.0 copy-done.1
  4.0 119.2 %shard_map.83 = (f32[160,1152]{1,0:T(8,128)S(1)}, f32[160,1152]{1,0:T(8,128)S(1)}, f32[8,128]{1,0:T(8,128)S(1)}) custom-call(f32[2]{0:T(128)S(1)} %pad_maximum_fusion.scale_ref, bf16[160,1152]{1,0:T(8,128)(2,1)S(1)} %copy-done, bf16[160,1152]{1,0:T(8,128)(2,1)S(1)} %copy-done.1), custom_call_target="tpu_custom_call" | custom-call | tf_op jit(solution)/shard_map/pallas_call | solution.py:203
  123.2 0.5 fusion
  123.7 0.9 copy.13
  124.6 0.9 copy.14
Async XLA Ops:
  2.0 1.0 copy-start
  3.0 1.0 copy-start.1

commit v2 on v1

v2 whole, which is shorter than its diff:
```python
import functools

import jax
import jax.numpy as jnp
from jax import lax
from jax.experimental import pallas as pl
from jax.experimental.pallas import tpu as pltpu
from jax.sharding import PartitionSpec as P

MESH = pl.DeviceIdType.MESH
SHIFTS = 4
EPS = 1e-06
RUN = 8
CHUNK = 32
WRAP = 0
SWAP = 0
REDUCE = (0, 0, 1, 2)
COLS = 384


def ring_stages(b, g, n_blk, n_group):
    x, zl = lax.div(b, RUN), lax.rem(b, RUN)
    y, low = lax.div(g, 4), lax.rem(g, 4)
    zh, core = lax.div(low, 2), lax.rem(low, 2)
    n_x, n_y = n_blk // RUN, n_group // 4
    z = zh * RUN + zl

    def along_z(k):
        other = lax.rem(z + k, 2 * RUN)
        return (x * RUN + lax.rem(other, RUN), y * 4 + lax.div(other, RUN) * 2 + core)

    return [
        (core, [(b, y * 4 + zh * 2 + (1 - core))]),
        (x, [(lax.rem(b + RUN * k, n_blk), g) for k in range(1, n_x)]),
        (y, [(b, lax.rem(g + 4 * k, n_group)) for k in range(1, n_y)]),
        (z, [along_z(k) for k in range(1, 2 * RUN)]),
    ]


def kernel(
    n_blk, n_group, images_hbm, texts_hbm, exponent_hbm, bias_hbm,
    gimg_ref, gtxt_ref, sums_ref,
    raw, exponent_ref, bias_ref, blocks, unit, length, grad, totals, parts,
    in_sem, send_sem, recv_sem, part_send, part_recv, ready, know_x, know_y, know_z,
):
    rows, width = images_hbm.shape
    n_chunks = rows // CHUNK
    b, g = lax.axis_index("blk"), lax.axis_index("group")
    right, left = lax.rem(b + 1, n_blk), lax.rem(b + n_blk - 1, n_blk)
    partner = lax.rem(g + n_group // 2, n_group)
    stages = ring_stages(b, g, n_blk, n_group)

    loads = [
        pltpu.make_async_copy(src, dst, in_sem.at[k])
        for k, (src, dst) in enumerate(
            ((texts_hbm, raw.at[0]), (images_hbm, raw.at[1]), (exponent_hbm, exponent_ref), (bias_hbm, bias_ref))
        )
    ]
    for load in loads:
        load.start()

    x, place = lax.div(b, RUN), lax.rem(b, RUN)
    low = lax.rem(g, 4)
    z_hi, core = lax.div(low, 2), lax.rem(low, 2)
    z, n_z = z_hi * RUN + place, 2 * RUN

    def at_x(k):
        return (lax.rem(b + k * RUN + n_blk, n_blk), g)

    def at_y(k):
        return (b, lax.rem(g + 4 * k + n_group, n_group))

    def at_z(k):
        return (x * RUN + lax.rem(z + k, RUN), g + 2 * (lax.div(z + k, RUN) - z_hi))

    def tell(semaphore, device):
        pl.semaphore_signal(semaphore, inc=1, device_id=device, device_id_type=MESH)

    def tell_z(semaphore, k):
        @pl.when(z >= k)
        def _():
            tell(semaphore, at_z(-k))

        @pl.when(z + k < n_z)
        def _():
            tell(semaphore, at_z(k))

    def heard_z(k):
        return jnp.where(z >= k, 1, 0) + jnp.where(z + k < n_z, 1, 0)

    barrier = pltpu.get_barrier_semaphore()
    for device in ((b, g + 1 - 2 * core), at_x(1), at_x(-1), at_y(1), at_y(-1)):
        tell(barrier, device)
    tell_z(barrier, 1)

    @pl.when(place == 0)
    def _():
        tell(barrier, (left, g))

    def prepare(stream):
        loads[stream].wait()
        widened = raw[stream].astype(jnp.float32)
        size = jnp.sqrt(jnp.sum(widened * widened, axis=-1, keepdims=True) + EPS)
        unit_rows = widened / size
        unit[stream] = unit_rows
        length[stream] = size
        blocks[stream, 0] = unit_rows.astype(jnp.bfloat16)

    prepare(0)
    totals[...] = jnp.zeros_like(totals)
    loads[2].wait()
    loads[3].wait()
    temperature = jnp.exp(jnp.broadcast_to(exponent_ref[0], (1, 1)))
    bias = bias_ref[0]

    def move(stream, hop, chunk):
        if hop == SHIFTS - 1:
            target = (b, partner)
        else:
            target = (right, g) if stream == 0 else (left, g)
        at = pl.ds(pl.multiple_of(chunk * CHUNK, CHUNK), CHUNK)
        return pltpu.make_async_remote_copy(
            src_ref=blocks.at[stream, hop, at],
            dst_ref=blocks.at[stream, hop + 1, at],
            send_sem=send_sem.at[stream, hop, chunk],
            recv_sem=recv_sem.at[stream, hop, chunk],
            device_id=target,
            device_id_type=MESH,
        )

    def meet(stream, hop, own, add):
        mine, block = blocks[1 - stream, 0], blocks[stream, hop]
        cosine = lax.dot_general(mine, block, (((1,), (1,)), ((), ())), preferred_element_type=jnp.float32)
        logits = temperature * cosine + bias
        if own:
            same = lax.broadcasted_iota(jnp.int32, (rows, rows), 0) == lax.broadcasted_iota(jnp.int32, (rows, rows), 1)
            sign = jnp.where(same, 1.0, -1.0)
            flipped = -sign * logits
        else:
            flipped = logits
        slope = jax.nn.sigmoid(flipped)
        if own:
            slope = -sign * slope
        weights = (temperature * slope).astype(jnp.bfloat16)
        for c in range(0, width, COLS):
            part = jnp.dot(weights, blocks[stream, hop, :, c : c + COLS], preferred_element_type=jnp.float32)
            if add:
                grad[1 - stream, :, c : c + COLS] += part
            else:
                grad[1 - stream, :, c : c + COLS] = part
        if stream == 1:
            return
        term = jnp.maximum(flipped, 0.0) + jnp.log1p(jnp.exp(-jnp.abs(flipped)))
        for i, value in enumerate((term, slope * (temperature * cosine), slope)):
            totals[i : i + 1, :] += jnp.sum(value, axis=0, keepdims=True)

    pl.semaphore_wait(barrier, 5 + heard_z(1) + jnp.where(place == RUN - 1, 1, 0))
    tell(ready, (right, g))
    for k in (1, -1):
        tell(know_x, at_x(k))
        tell(know_y.at[0], at_y(k))
    tell_z(know_z.at[0], 1)

    def lag(stream, hop):
        before = place if stream == 0 else RUN - 1 - place
        ring = min(hop, SHIFTS - 1)
        late = jnp.where(before < ring, 1, 0)
        return hop + late * WRAP + (SWAP if hop == SHIFTS else 0), late

    def reduce_stage(s):
        index, line = stages[s]
        if s == len(stages) - 1:
            pl.semaphore_wait(know_z.at[3], heard_z(8))
        if s == 0:
            value = jnp.broadcast_to(jnp.sum(totals[...], axis=1, keepdims=True), (8, 128))
        else:
            value = collect(s - 1)
        parts[s, index] = value
        for copy in part_copies(s):
            copy.start()

    def part_copies(s):
        index, line = stages[s]
        first = sum(len(stages[i][1]) for i in range(s))
        return [
            pltpu.make_async_remote_copy(
                src_ref=parts.at[s, index],
                dst_ref=parts.at[s, index],
                send_sem=part_send.at[first + k],
                recv_sem=part_recv.at[first + k],
                device_id=peer,
                device_id_type=MESH,
            )
            for k, peer in enumerate(line)
        ]

    def collect(s):
        for copy in part_copies(s):
            copy.wait_recv()
        value = parts[s, 0]
        for i in range(1, len(stages[s][1]) + 1):
            value = value + parts[s, i]
        return value

    def finish(stream, out):
        gradient, unit_rows = grad[stream], unit[stream]
        along = jnp.sum(unit_rows * gradient, axis=-1, keepdims=True)
        out[...] = (gradient - unit_rows * along) / length[stream]

    def round_of(r, carry):
        for stream in (0, 1):
            chunk = r - stream * n_chunks

            @pl.when((chunk >= 0) & (chunk < n_chunks))
            def _():
                move(stream, 0, chunk).start()

        @pl.when(r == 1)
        def _():
            pl.semaphore_wait(know_x, 2)
            pl.semaphore_wait(know_y.at[0], 2)
            pl.semaphore_wait(know_z.at[0], heard_z(1))
            for k in (2, -2):
                tell(know_y.at[1], at_y(k))
            tell_z(know_z.at[1], 2)

        @pl.when(r == 2)
        def _():
            pl.semaphore_wait(know_y.at[1], 2)
            pl.semaphore_wait(know_z.at[1], heard_z(2))
            tell_z(know_z.at[2], 4)

        @pl.when(r == 3)
        def _():
            pl.semaphore_wait(know_z.at[2], heard_z(4))
            tell_z(know_z.at[3], 8)

        @pl.when(r == n_chunks - 1)
        def _():
            pl.semaphore_wait(ready, 1)

        for want in (0, 1):
            for stream in (0, 1):
                for hop in range(1, SHIFTS):
                    rounds, late = lag(stream, hop)
                    chunk = r - stream * n_chunks - rounds

                    @pl.when((chunk >= 0) & (chunk < n_chunks) & (late == want))
                    def _():
                        move(stream, hop - 1, chunk).wait_recv()
                        move(stream, hop, chunk).start()

        @pl.when(r == 0)
        def _():
            prepare(1)
            meet(0, 0, True, False)
            meet(1, 0, True, False)

        for stream in (0, 1):
            for hop in range(1, SHIFTS + 1):
                rounds, _ = lag(stream, hop)

                @pl.when(r == (stream + 1) * n_chunks - 1 + rounds)
                def _():
                    if hop == SHIFTS:
                        def arrived(chunk, c):
                            move(stream, hop - 1, chunk).wait_recv()
                            return c

                        lax.fori_loop(0, n_chunks, arrived, 0)
                    meet(stream, hop, False, True)

        for s in range(len(stages)):

            @pl.when(r == reduce_at + REDUCE[s])
            def _():
                reduce_stage(s)

        @pl.when(r == reduce_at + 1)
        def _():
            finish(1, gimg_ref)

        return carry

    reduce_at = n_chunks - 1 + SHIFTS + WRAP + SWAP
    n_rounds = 2 * n_chunks + SHIFTS + WRAP + SWAP
    assert reduce_at + REDUCE[-1] < n_rounds
    lax.fori_loop(0, n_rounds, round_of, 0)

    finish(0, gtxt_ref)
    count = n_blk * n_group * rows * (SHIFTS + 1) * rows
    sums_ref[...] = collect(len(stages) - 1) / count

    def sent(chunk, carry):
        for stream in (0, 1):
            for hop in range(SHIFTS):
                move(stream, hop, chunk).wait_send()
        return carry

    lax.fori_loop(0, n_chunks, sent, 0)
    for s in range(len(stages)):
        for copy in part_copies(s):
            copy.wait_send()


def solution(mesh):
    n_blk, n_group = mesh.shape["blk"], mesh.shape["group"]

    def body(images, texts, exponent_of_multiplier, bias):
        rows, width = images.shape
        n_chunks = rows // CHUNK
        n_parts = 1 + (n_blk // RUN - 1) + (n_group // 4 - 1) + (2 * RUN - 1)
        vmem = pl.BlockSpec(memory_space=pltpu.VMEM)
        grad_images, grad_texts, sums = pl.pallas_call(
            functools.partial(kernel, n_blk, n_group),
            out_shape=[
                jax.ShapeDtypeStruct((rows, width), jnp.float32),
                jax.ShapeDtypeStruct((rows, width), jnp.float32),
                jax.ShapeDtypeStruct((8, 128), jnp.float32),
            ],
            in_specs=[pl.BlockSpec(memory_space=pl.ANY)] * 4,
            out_specs=[vmem, vmem, vmem],
            scratch_shapes=[
                pltpu.VMEM((2, rows, width), jnp.bfloat16),
                pltpu.SMEM((1,), jnp.float32),
                pltpu.SMEM((1,), jnp.float32),
                pltpu.VMEM((2, SHIFTS + 1, rows, width), jnp.bfloat16),
                pltpu.VMEM((2, rows, width), jnp.float32),
                pltpu.VMEM((2, rows, 1), jnp.float32),
                pltpu.VMEM((2, rows, width), jnp.float32),
                pltpu.VMEM((8, rows), jnp.float32),
                pltpu.VMEM((4, 2 * RUN, 8, 128), jnp.float32),
                pltpu.SemaphoreType.DMA((4,)),
                pltpu.SemaphoreType.DMA((2, SHIFTS, n_chunks)),
                pltpu.SemaphoreType.DMA((2, SHIFTS, n_chunks)),
                pltpu.SemaphoreType.DMA((n_parts,)),
                pltpu.SemaphoreType.DMA((n_parts,)),
                pltpu.SemaphoreType.REGULAR,
                pltpu.SemaphoreType.REGULAR,
                pltpu.SemaphoreType.REGULAR((2,)),
                pltpu.SemaphoreType.REGULAR((4,)),
            ],
            compiler_params=pltpu.CompilerParams(
                collective_id=0, has_side_effects=True, vmem_limit_bytes=48 * 2**20
            ),
        )(images, texts, exponent_of_multiplier, bias)
        return grad_images, grad_texts, sums[0, 0:1], sums[1, 0:1], sums[2, 0:1]

    in_specs = (P(("blk", "group"), None), P(("blk", "group"), None), P(), P())
    out_specs = (P(("blk", "group"), None), P(("blk", "group"), None), P(), P(), P())
    return jax.shard_map(body, mesh=mesh, in_specs=in_specs, out_specs=out_specs, check_vma=False)
```

time: 126 us -> 93.2 us (0.74)
  Pallas kernels: 119 us -> 86.1 us
    pallas_call x1, Pallas kernels: 119 us -> 86.1 us  [body(): pl.pallas_call(functools.partial(kernel, n_blk, n_group), out_shape=[jax....]
where the time goes in v2:
time: 93.2 us; the launch traced here: 92.2 us
  Pallas kernels  86.1 us (92%)
  local copies, waits for them, and re-layouts  4.21 us (5%)
  between operations  1.94 us (2%)
    pallas_call x1, Pallas kernels, body(): pl.pallas_call(functools.partial(kernel, n_blk, n_group), out_shape=[jax....  86.1 us
    unnamed x6, local copies, waits for them, and re-layouts  3.69 us

profile of v2, /device:TPU:1, one launch (start us, length us, event | category | flops | bytes accessed | tf_op | source)
XLA Modules:
  0.0 92.2 jit_solution(1672584916474765492)
XLA Ops:
  1.9 0.0 copy-start
  1.9 1.0 %copy-done = bf16[160,1152]{1,0:T(8,128)(2,1)S(1)} copy-done((bf16[160,1152]{1,0:T(8,128)(2,1)S(1)}, bf16[160,1152]{1,0:T(8,128)(2,1)}, u32[]{:S(2)}) %copy-start) | copy-done | bytes 368664
  2.9 0.0 copy-start.1
  2.9 1.0 %copy-done.1 = bf16[160,1152]{1,0:T(8,128)(2,1)S(1)} copy-done((bf16[160,1152]{1,0:T(8,128)(2,1)S(1)}, bf16[160,1152]{1,0:T(8,128)(2,1)}, u32[]{:S(2)}) %copy-start.1) | copy-done | bytes 368664
  3.9 86.1 %shard_map.83 = (f32[160,1152]{1,0:T(8,128)S(1)}, f32[160,1152]{1,0:T(8,128)S(1)}, f32[8,128]{1,0:T(8,128)S(1)}) custom-call(bf16[160,1152]{1,0:T(8,128)(2,1)S(1)} %copy-done, bf16[160,1152]{1,0:T(8,128)(2,1)S(1)} %copy-done.1, f32[1]{0:T(128)S(6)} %copy.11.exponent_hbm, f32[1]{0:T(128)S(6)} %copy.12.bias_hbm), custom_call_target="tpu_custom_call" | custom-call | tf_op jit(solution)/shard_map/pallas_call | solution.py:314
  90.0 0.5 fusion
  90.5 0.9 copy.13
  91.4 0.9 copy.14
Async XLA Ops:
  1.9 1.0 %copy-start = (bf16[160,1152]{1,0:T(8,128)(2,1)S(1)}, bf16[160,1152]{1,0:T(8,128)(2,1)}, u32[]{:S(2)}) copy-start(bf16[160,1152]{1,0:T(8,128)(2,1)} %images_hbm.1) | copy-start | bytes 1105924
  2.9 1.0 %copy-start.1 = (bf16[160,1152]{1,0:T(8,128)(2,1)S(1)}, bf16[160,1152]{1,0:T(8,128)(2,1)}, u32[]{:S(2)}) copy-start(bf16[160,1152]{1,0:T(8,128)(2,1)} %texts_hbm.1) | copy-start | bytes 1105924

commit v3 on v2

--- a/solution.py
+++ b/solution.py
@@ -14,7 +14,7 @@
 CHUNK = 32
 WRAP = 0
 SWAP = 0
-REDUCE = (0, 0, 1, 2)
+REDUCE = (0, 1, 2)
 COLS = 384
 
 
@@ -30,35 +30,33 @@
         return (x * RUN + lax.rem(other, RUN), y * 4 + lax.div(other, RUN) * 2 + core)
 
     return [
-        (core, [(b, y * 4 + zh * 2 + (1 - core))]),
-        (x, [(lax.rem(b + RUN * k, n_blk), g) for k in range(1, n_x)]),
+        (
+            x * 2 + core,
+            [
+                (lax.rem(b + RUN * k, n_blk), g + flip * (1 - 2 * core))
+                for flip in (0, 1)
+                for k in range(n_x)
+                if (flip, k) != (0, 0)
+            ],
+        ),
         (y, [(b, lax.rem(g + 4 * k, n_group)) for k in range(1, n_y)]),
         (z, [along_z(k) for k in range(1, 2 * RUN)]),
     ]
 
 
 def kernel(
-    n_blk, n_group, images_hbm, texts_hbm, exponent_hbm, bias_hbm,
+    n_blk, n_group, images_ref, texts_ref, exponent_ref, bias_ref,
     gimg_ref, gtxt_ref, sums_ref,
-    raw, exponent_ref, bias_ref, blocks, unit, length, grad, totals, parts,
-    in_sem, send_sem, recv_sem, part_send, part_recv, ready, know_x, know_y, know_z,
+    blocks, unit, length, grad, totals, parts,
+    send_sem, recv_sem, part_send, part_recv, ready, know_core, know_x, know_y, know_z,
 ):
-    rows, width = images_hbm.shape
+    rows, width = images_ref.shape
     n_chunks = rows // CHUNK
     b, g = lax.axis_index("blk"), lax.axis_index("group")
     right, left = lax.rem(b + 1, n_blk), lax.rem(b + n_blk - 1, n_blk)
     partner = lax.rem(g + n_group // 2, n_group)
     stages = ring_stages(b, g, n_blk, n_group)
 
-    loads = [
-        pltpu.make_async_copy(src, dst, in_sem.at[k])
-        for k, (src, dst) in enumerate(
-            ((texts_hbm, raw.at[0]), (images_hbm, raw.at[1]), (exponent_hbm, exponent_ref), (bias_hbm, bias_ref))
-        )
-    ]
-    for load in loads:
-        load.start()
-
     x, place = lax.div(b, RUN), lax.rem(b, RUN)
     low = lax.rem(g, 4)
     z_hi, core = lax.div(low, 2), lax.rem(low, 2)
@@ -98,8 +96,7 @@
         tell(barrier, (left, g))
 
     def prepare(stream):
-        loads[stream].wait()
-        widened = raw[stream].astype(jnp.float32)
+        widened = (texts_ref, images_ref)[stream][...].astype(jnp.float32)
         size = jnp.sqrt(jnp.sum(widened * widened, axis=-1, keepdims=True) + EPS)
         unit_rows = widened / size
         unit[stream] = unit_rows
@@ -108,8 +105,6 @@
 
     prepare(0)
     totals[...] = jnp.zeros_like(totals)
-    loads[2].wait()
-    loads[3].wait()
     temperature = jnp.exp(jnp.broadcast_to(exponent_ref[0], (1, 1)))
     bias = bias_ref[0]
 
@@ -218,6 +213,7 @@
         @pl.when(r == 1)
         def _():
             pl.semaphore_wait(know_x, 2)
+            tell(know_core, (b, g + 1 - 2 * core))
             pl.semaphore_wait(know_y.at[0], 2)
             pl.semaphore_wait(know_z.at[0], heard_z(1))
             for k in (2, -2):
@@ -226,6 +222,7 @@
 
         @pl.when(r == 2)
         def _():
+            pl.semaphore_wait(know_core, 1)
             pl.semaphore_wait(know_y.at[1], 2)
             pl.semaphore_wait(know_z.at[1], heard_z(2))
             tell_z(know_z.at[2], 4)
@@ -309,7 +306,7 @@
     def body(images, texts, exponent_of_multiplier, bias):
         rows, width = images.shape
         n_chunks = rows // CHUNK
-        n_parts = 1 + (n_blk // RUN - 1) + (n_group // 4 - 1) + (2 * RUN - 1)
+        n_parts = (2 * (n_blk // RUN) - 1) + (n_group // 4 - 1) + (2 * RUN - 1)
         vmem = pl.BlockSpec(memory_space=pltpu.VMEM)
         grad_images, grad_texts, sums = pl.pallas_call(
             functools.partial(kernel, n_blk, n_group),
@@ -318,23 +315,20 @@
                 jax.ShapeDtypeStruct((rows, width), jnp.float32),
                 jax.ShapeDtypeStruct((8, 128), jnp.float32),
             ],
-            in_specs=[pl.BlockSpec(memory_space=pl.ANY)] * 4,
+            in_specs=[vmem, vmem, pl.BlockSpec(memory_space=pltpu.SMEM), pl.BlockSpec(memory_space=pltpu.SMEM)],
             out_specs=[vmem, vmem, vmem],
             scratch_shapes=[
-                pltpu.VMEM((2, rows, width), jnp.bfloat16),
-                pltpu.SMEM((1,), jnp.float32),
-                pltpu.SMEM((1,), jnp.float32),
                 pltpu.VMEM((2, SHIFTS + 1, rows, width), jnp.bfloat16),
                 pltpu.VMEM((2, rows, width), jnp.float32),
                 pltpu.VMEM((2, rows, 1), jnp.float32),
                 pltpu.VMEM((2, rows, width), jnp.float32),
                 pltpu.VMEM((8, rows), jnp.float32),
-                pltpu.VMEM((4, 2 * RUN, 8, 128), jnp.float32),
-                pltpu.SemaphoreType.DMA((4,)),
+                pltpu.VMEM((3, 2 * RUN, 8, 128), jnp.float32),
                 pltpu.SemaphoreType.DMA((2, SHIFTS, n_chunks)),
                 pltpu.SemaphoreType.DMA((2, SHIFTS, n_chunks)),
                 pltpu.SemaphoreType.DMA((n_parts,)),
                 pltpu.SemaphoreType.DMA((n_parts,)),
+                pltpu.SemaphoreType.REGULAR,
                 pltpu.SemaphoreType.REGULAR,
                 pltpu.SemaphoreType.REGULAR,
                 pltpu.SemaphoreType.REGULAR((2,)),

time: 93.2 us -> 93 us (level)
  no operation moved by 1% of the time
where the time goes in v3:
time: 93 us; the launch traced here: 92.7 us
  Pallas kernels  86.6 us (93%)
  local copies, waits for them, and re-layouts  4.21 us (5%)
  between operations  1.94 us (2%)
    pallas_call x1, Pallas kernels, body(): pl.pallas_call(functools.partial(kernel, n_blk, n_group), out_shape=[jax....  86.6 us
    unnamed x6, local copies, waits for them, and re-layouts  3.69 us

profile of v3, /device:TPU:1, one launch (start us, length us, event | category | flops | bytes accessed | tf_op | source)
XLA Modules:
  0.0 92.7 jit_solution(16095452748751917611)
XLA Ops:
  1.9 0.0 copy-start
  1.9 1.0 %copy-done = bf16[160,1152]{1,0:T(8,128)(2,1)S(1)} copy-done((bf16[160,1152]{1,0:T(8,128)(2,1)S(1)}, bf16[160,1152]{1,0:T(8,128)(2,1)}, u32[]{:S(2)}) %copy-start) | copy-done | bytes 368664
  2.9 0.0 copy-start.1
  2.9 1.0 %copy-done.1 = bf16[160,1152]{1,0:T(8,128)(2,1)S(1)} copy-done((bf16[160,1152]{1,0:T(8,128)(2,1)S(1)}, bf16[160,1152]{1,0:T(8,128)(2,1)}, u32[]{:S(2)}) %copy-start.1) | copy-done | bytes 368664
  3.9 86.6 %shard_map.83 = (f32[160,1152]{1,0:T(8,128)S(1)}, f32[160,1152]{1,0:T(8,128)S(1)}, f32[8,128]{1,0:T(8,128)S(1)}) custom-call(bf16[160,1152]{1,0:T(8,128)(2,1)S(1)} %copy-done, bf16[160,1152]{1,0:T(8,128)(2,1)S(1)} %copy-done.1, f32[1]{0:T(128)S(6)} %copy.11.exponent_ref, f32[1]{0:T(128)S(6)} %copy.12.bias_ref), custom_call_target="tpu_custom_call" | custom-call | tf_op jit(solution)/shard_map/pallas_call | solution.py:311
  90.5 0.5 fusion
  91.0 0.9 copy.13
  91.9 0.9 copy.14
Async XLA Ops:
  1.9 1.0 %copy-start = (bf16[160,1152]{1,0:T(8,128)(2,1)S(1)}, bf16[160,1152]{1,0:T(8,128)(2,1)}, u32[]{:S(2)}) copy-start(bf16[160,1152]{1,0:T(8,128)(2,1)} %images_ref.1) | copy-start | bytes 1105924
  2.9 1.0 %copy-start.1 = (bf16[160,1152]{1,0:T(8,128)(2,1)S(1)}, bf16[160,1152]{1,0:T(8,128)(2,1)}, u32[]{:S(2)}) copy-start(bf16[160,1152]{1,0:T(8,128)(2,1)} %texts_ref.1) | copy-start | bytes 1105924
